TPU v7x, 32 devices: a whole 2x2x4 slice. The times are simulated.
32 devices in a mesh: groups: 2 (over x), store: 8 (over z, y), tensor: 2 (over core).
Axes of the slice: x: 2, y: 2, z: 4, core: 2. Of those that a mesh axis runs over, the one named last changes fastest.
Arguments:
- hidden_in: bfloat16 [6144, 8192], P(('groups', 'store'), 'tensor'), parts along dimension 0, may hold values from -6 to 6
- base_weight: bfloat16 [8192, 1024], P('tensor'), may hold values from -0.0625 to 0.0625
- adapter_down: bfloat16 [32, 8192, 64], P(('groups', 'store'), 'tensor'), parts along dimension 0, may hold values from -0.0625 to 0.0625
- adapter_up: bfloat16 [32, 64, 1024], P(('groups', 'store')), parts along dimension 0, may hold values from -0.75 to 0.75
- lengths: int32 [768], P(('groups', 'store')), parts along dimension 0, may hold values from 1 to 15, as said below
- adapter_ids: int32 [768], P(('groups', 'store')), parts along dimension 0, may hold values from 0 to 15, as said below
Outputs:
- key_proj: bfloat16 [6144, 1024], P(('groups', 'store'), 'tensor'), parts along dimension 0
There are 2 independent parts, one for each index of `groups`. A program takes and returns all parts, laid end to end along the dimension named above; an argument that names none is the same for every part. Nothing has to cross between parts.
Inputs may be any that keep to these rules, and one draw needn't show every extreme that they name: The lengths of the requests of one store index sum to 384. The owner of adapter a is store index a // 2; the requests of one store index send at most 90 tokens to the adapters of one owner, and some owner gets exactly 90 from every store index. `adapter_ids`: adapter of each request, owned as stated for lengths.
All inputs are finite; a program needn't handle non-finite values.
Results may differ from a plain program's by a relative error of at most 0.012.
Values may be sent and summed in bfloat16 or wider, within the bound.
A program may use at most 128 MiB of HBM per device.

v0:
```python
import jax
import jax.numpy as jnp
from jax import lax
from jax.sharding import PartitionSpec as P

LONGEST_LENGTH = 15


adapter_scale = 0.5


def local(hidden_in, base_weight, adapter_down, adapter_up, lengths, adapter_ids):
    store_count_total = lax.axis_size("store")
    token_count = hidden_in.shape[0]
    feature_half = hidden_in.shape[1]
    request_count = lengths.shape[0]
    adapters_here = adapter_down.shape[0]
    rank_size = adapter_down.shape[2]
    width_out = adapter_up.shape[2]
    store_capacity = LONGEST_LENGTH * ((request_count + store_count_total - 1) // store_count_total)
    request_ends = jnp.cumsum(lengths)
    request_starts = request_ends - lengths
    owners = adapter_ids // adapters_here
    local_pick = adapter_ids % adapters_here
    positions = jnp.arange(request_count, dtype=jnp.int32)
    earlier = (owners[:, None] == owners[None, :]) & (positions[None, :] < positions[:, None])
    first_slot = jnp.sum(jnp.where(earlier, lengths[None, :], 0), axis=1)
    token_index = jnp.arange(token_count, dtype=jnp.int32)
    request = jnp.sum((request_ends[None, :] <= token_index[:, None]).astype(jnp.int32), axis=1)
    destination_store = (
        owners[request] * store_capacity
        + first_slot[request]
        + token_index
        - request_starts[request]
    )
    slot_index = jnp.arange(store_count_total * store_capacity, dtype=jnp.int32)
    matches = destination_store[None, :] == slot_index[:, None]
    filled = jnp.any(matches, axis=1)
    source = jnp.sum(jnp.where(matches, token_index[None, :], 0), axis=1)
    outgoing = jnp.where(filled[:, None], hidden_in[source], jnp.zeros((), hidden_in.dtype))
    outgoing = outgoing.reshape(store_count_total, store_capacity, feature_half)
    slot_labels = jnp.where(filled, local_pick[request[source]], 0).reshape(
        store_count_total, store_capacity
    )
    down_flat = adapter_down.transpose(1, 0, 2).reshape(feature_half, adapters_here * rank_size)
    up_flat = adapter_up.reshape(adapters_here * rank_size, width_out).astype(jnp.float32)
    column_owner = jnp.arange(adapters_here * rank_size, dtype=jnp.int32) // rank_size
    slot_rows = lax.all_to_all(outgoing, "store", split_axis=0, concat_axis=0, tiled=True)
    labels = lax.all_to_all(slot_labels, "store", split_axis=0, concat_axis=0, tiled=True)
    item_count = slot_rows.shape[1]
    projected = jnp.dot(
        slot_rows.reshape(-1, feature_half), down_flat, preferred_element_type=jnp.float32
    )
    chosen = jnp.where(column_owner[None, :] == labels.reshape(-1)[:, None], projected, 0.0)
    chosen = lax.psum(chosen.astype(jnp.bfloat16), "tensor").astype(jnp.float32)
    column_count = width_out // lax.axis_size("tensor")
    part_up = lax.dynamic_slice_in_dim(
        up_flat, lax.axis_index("tensor") * column_count, column_count, 1
    )
    adapter_out = jnp.dot(
        chosen, part_up, precision=lax.Precision.HIGHEST, preferred_element_type=jnp.float32
    )
    adapter_out = adapter_out.astype(jnp.bfloat16)
    gathered_back = lax.all_to_all(
        adapter_out.reshape(store_count_total, item_count, -1),
        "store",
        split_axis=0,
        concat_axis=0,
        tiled=True,
    )
    adapter_token_rows = gathered_back.reshape(store_count_total * store_capacity, -1)[
        destination_store
    ].astype(jnp.float32)
    base_projection = jnp.dot(hidden_in, base_weight, preferred_element_type=jnp.float32)
    summed_out = lax.psum_scatter(
        base_projection.astype(jnp.bfloat16), "tensor", scatter_dimension=1, tiled=True
    ).astype(jnp.float32)
    summed_out = summed_out + adapter_scale * adapter_token_rows
    return summed_out.astype(jnp.bfloat16)


def solution(mesh):
    return jax.shard_map(
        local,
        mesh=mesh,
        in_specs=(
            P(("groups", "store"), "tensor"),
            P("tensor", None),
            P(("groups", "store"), "tensor", None),
            P(("groups", "store"), None, None),
            P(("groups", "store")),
            P(("groups", "store")),
        ),
        out_specs=P(("groups", "store"), "tensor"),
        check_vma=False,
    )
```

profile of v0, /device:TPU:0, one launch (start us, length us, event | category | flops | bytes accessed | tf_op | source)
XLA Modules:
  0.0 386.0 jit_solution(17829293991312189326)
XLA Ops:
  6.5 0.8 and_select_fusion
  8.0 0.8 select_reduce_fusion.1
  8.9 0.7 copy.9
  11.2 0.7 fusion.17
  12.0 0.7 fusion.18
  12.7 0.7 fusion.14
  13.4 0.7 fusion.15
  14.8 0.7 fusion.11
  15.6 0.7 fusion.12
  16.3 4.3 %select_reduce_fusion.3 = (s32[384]{0:T(512)S(1)}, s32[384,1]{0,1:T(1,128)S(1)}) fusion(s32[]{:T(128)} %bitcast.90, s32[]{:T(128)} %bitcast.91, s32[]{:T(128)} %bitcast.92, s32[]{:T(128)} %bitcast.93, s32[]{:T(128)} %bitcast.94, s32[]{:T(128)} %bitcast.96, s32[]{:T(128)} %bitcast.95, s32[384]{0:T(512)S(1)} %convert_reduce_fusion), kind=kLoop, calls=%fused_computation.124 | loop fusion | flops 5760 | bytes 4636 | tf_op jit(solution)/shard_map/gather | solution.py:32
  20.8 8.7 %select_reduce_fusion.4 = (s32[384]{0:T(512)S(1)}, s32[384]{0:T(512)S(1)}) fusion(s32[]{:T(128)} %bitcast.42, s32[]{:T(128)} %bitcast.43, s32[]{:T(128)} %bitcast.44, s32[]{:T(128)} %bitcast.45, s32[]{:T(128)} %bitcast.46, s32[]{:T(128)} %bitcast.48, s32[]{:T(128)} %bitcast.47, s32[384,1]{0,1:T(1,128)S(1)} %get-tuple-element.95, s32[]{:T(128)} %bitcast.144, ...), kind=kLoop, calls=%fused_computation.125 | loop fusion | flops 6912 | bytes 4664 | tf_op jit(solution)/shard_map/gather | solution.py:31
  29.5 76.9 %add_subtract_fusion = (s32[384]{0:T(512)S(1)}, s32[384]{0:T(512)S(1)}, s32[384]{0:T(512)S(1)}) fusion(pred[384]{0:T(512)(128)(4,1)S(1)} %get-tuple-element.88, pred[384]{0:T(512)(128)(4,1)S(1)} %get-tuple-element.87, pred[384]{0:T(512)(128)(4,1)S(1)} %get-tuple-element.84, pred[384]{0:T(512)(128)(4,1)S(1)} %get-tuple-element.85, ...), kind=kLoop, calls=%fused_computation.118 | loop fusion | flops 48768 | bytes 25452 | tf_op jit(solution)/shard_map/sub | solution.py:31
  109.0 5.0 %gather_fusion = s32[720]{0:T(1024)S(1)} fusion(s32[384]{0:T(512)S(1)} %convert_reduce_fusion, s32[1024]{0:T(1024)S(1)} %pad_clamp_fusion.1), kind=kCustom, calls=%fused_computation | custom fusion | bytes 8640 | tf_op jit(solution)/shard_map/gather | solution.py:42
  114.0 4.3 %fusion.4 = (s32[720]{0:T(1024)S(1)}, s32[720,1]{0,1:T(1,128)S(1)}) fusion(s32[]{:T(128)} %bitcast.186, s32[]{:T(128)} %bitcast.187, s32[]{:T(128)} %bitcast.188, s32[]{:T(128)} %bitcast.189, s32[]{:T(128)} %bitcast.190, s32[]{:T(128)} %bitcast.192, s32[]{:T(128)} %bitcast.191, s32[720]{0:T(1024)S(1)} %gather_fusion), kind=kLoop, calls=%fused_computation.113 | loop fusion | flops 10800 | bytes 8668 | tf_op jit(solution)/shard_map/gather | solution.py:42
  118.7 25.8 %select_select_fusion = s32[720]{0:T(1024)S(1)} fusion(pred[720]{0:T(1024)(128)(4,1)S(1)} %fusion.1, pred[720]{0:T(1024)(128)(4,1)S(1)} %get-tuple-element.45, pred[720]{0:T(1024)(128)(4,1)S(1)} %get-tuple-element.44, pred[720]{0:T(1024)(128)(4,1)S(1)} %get-tuple-element.43, pred[720]{0:T(1024)(128)(4,1)S(1)} %get-tuple-element.42, ...), kind=kLoop, calls=%fused_computation.112 | loop fusion | flops 30240 | bytes 36164 | tf_op jit(solution)/shard_map/jit(_where)/select_n | solution.py:42
  145.2 7.3 %all-to-all-start = ((s32[8,1,90]{2,1,0:T(1,128)}), s32[8,1,90]{2,1,0:T(1,128)S(1)}, u32[]{:S(2)}, u32[]{:S(2)}) async-start(s32[8,1,90]{2,1,0:T(1,128)} %select_n.108), calls=%async_computation.1 | async-start | bytes 8192 | tf_op jit(solution)/shard_map/all_to_all | solution.py:49
  152.5 5.6 %gather_fusion.1 = bf16[720,4096]{1,0:T(8,128)(2,1)} fusion(bf16[384,4096]{1,0:T(8,128)(2,1)S(1)} %copy-done, s32[1024]{0:T(1024)S(1)} %pad_clamp_fusion.1), kind=kCustom, calls=%fused_computation.1 | custom fusion | bytes 11799360 | tf_op jit(solution)/shard_map/gather | solution.py:40
  158.1 5.3 %gather.34 = bf16[8,90,4096]{2,1,0:T(8,128)(2,1)} reshape(bf16[720,4096]{1,0:T(8,128)(2,1)} %gather_fusion.1) | data formatting | bytes 11796480 | tf_op jit(solution)/shard_map/gather | solution.py:40
  163.4 5.9 %broadcast_select_fusion = bf16[8,90,4096]{2,1,0:T(8,128)(2,1)} fusion(bf16[8,90,4096]{2,1,0:T(8,128)(2,1)} %gather.34, pred[8,90]{1,0:T(8,128)(4,1)S(1)} %broadcast_in_dim.67), kind=kLoop, calls=%fused_computation.3 | loop fusion | flops 2949120 | bytes 11797200 | tf_op jit(solution)/shard_map/jit(_where)/select_n | solution.py:40
  169.3 6.0 %all-to-all-start.1 = ((bf16[8,90,4096]{2,1,0:T(8,128)(2,1)}), bf16[8,90,4096]{2,1,0:T(8,128)(2,1)}, u32[]{:S(2)}, u32[]{:S(2)}) async-start(bf16[8,90,4096]{2,1,0:T(8,128)(2,1)} %broadcast_select_fusion), calls=%async_computation.2 | async-start | bytes 12582912 | tf_op jit(solution)/shard_map/all_to_all | solution.py:48
  176.7 136.4 %all-to-all-done.1 = bf16[8,90,4096]{2,1,0:T(8,128)(2,1)} async-done(((bf16[8,90,4096]{2,1,0:T(8,128)(2,1)}), bf16[8,90,4096]{2,1,0:T(8,128)(2,1)}, u32[]{:S(2)}, u32[]{:S(2)}) %all-to-all-start.1) | async-done | bytes 5898272 | tf_op jit(solution)/shard_map/all_to_all | solution.py:48
  313.0 5.2 %reshape.182 = bf16[720,4096]{1,0:T(8,128)(2,1)} reshape(bf16[8,90,4096]{2,1,0:T(8,128)(2,1)} %all-to-all-done.1) | data formatting | bytes 11796480 | tf_op jit(solution)/shard_map/reshape | solution.py:52
  318.2 5.3 %fusion = bf16[720,128]{1,0:T(8,128)(2,1)} fusion(bf16[720,4096]{1,0:T(8,128)(2,1)} %reshape.182, bf16[4096,128]{0,1:T(8,128)(2,1)} %bitcast.204, s32[128]{0:T(128)S(1)} %and_select_fusion.2, s32[720]{0:T(1024)S(1)} %eq.50), kind=kOutput, calls=%fused_computation.7 | convolution fusion | flops 755251200 | bytes 7134528 | tf_op jit(solution)/shard_map/dot_general | solution.py:51
  323.6 6.8 %convolution_convert_fusion = bf16[384,1024]{1,0:T(8,128)(2,1)} fusion(bf16[384,4096]{1,0:T(8,128)(2,1)S(1)} %copy-done, bf16[4096,1024]{1,0:T(8,128)(2,1)} %param.7), kind=kOutput, calls=%fused_computation.4 | convolution fusion | flops 3221618688 | bytes 12320768 | tf_op jit(solution)/shard_map/dot_general | solution.py:74
  330.5 10.3 %all-reduce.2.cloned.1.call-done = bf16[720,128]{1,0:T(8,128)(2,1)} async-done(((bf16[720,128]{1,0:T(8,128)(2,1)}), bf16[720,128]{1,0:T(8,128)(2,1)}) %all-reduce.2.cloned.1.call-update) | async-done | bytes 184336 | tf_op jit(solution)/shard_map/psum | solution.py:55
  340.8 2.1 convolution_convert_fusion.1
  343.0 2.2 reshape.185
  345.2 5.8 %all-to-all-start.2 = ((bf16[8,90,512]{2,1,0:T(8,128)(2,1)}), bf16[8,90,512]{2,1,0:T(8,128)(2,1)}, u32[]{:S(2)}, u32[]{:S(2)}) async-start(bf16[8,90,512]{2,1,0:T(8,128)(2,1)} %reshape.185), calls=%async_computation.3 | async-start | bytes 1572864 | tf_op jit(solution)/shard_map/all_to_all | solution.py:64
  351.0 20.7 %all-to-all-done.2 = bf16[8,90,512]{2,1,0:T(8,128)(2,1)} async-done(((bf16[8,90,512]{2,1,0:T(8,128)(2,1)}), bf16[8,90,512]{2,1,0:T(8,128)(2,1)}, u32[]{:S(2)}, u32[]{:S(2)}) %all-to-all-start.2) | async-done | bytes 737312 | tf_op jit(solution)/shard_map/all_to_all | solution.py:64
  371.7 2.2 reshape.186
  373.9 3.3 gather_fusion.2
  377.2 1.9 add_convert_fusion
  (34 shorter events, 8.3 us)
Async XLA Ops:
  6.5 146.0 %copy-start = (bf16[384,4096]{1,0:T(8,128)(2,1)S(1)}, bf16[384,4096]{1,0:T(8,128)(2,1)}, u32[]{:S(2)}) copy-start(bf16[384,4096]{1,0:T(8,128)(2,1)} %param.6) | copy-start | bytes 9437188
  145.2 24.2 %all-to-all-start = ((s32[8,1,90]{2,1,0:T(1,128)}), s32[8,1,90]{2,1,0:T(1,128)S(1)}, u32[]{:S(2)}, u32[]{:S(2)}) async-start(s32[8,1,90]{2,1,0:T(1,128)} %select_n.108), calls=%async_computation.1 | async-start | bytes 8192 | tf_op jit(solution)/shard_map/all_to_all | solution.py:49
  169.3 143.7 %all-to-all-start.1 = ((bf16[8,90,4096]{2,1,0:T(8,128)(2,1)}), bf16[8,90,4096]{2,1,0:T(8,128)(2,1)}, u32[]{:S(2)}, u32[]{:S(2)}) async-start(bf16[8,90,4096]{2,1,0:T(8,128)(2,1)} %broadcast_select_fusion), calls=%async_computation.2 | async-start | bytes 12582912 | tf_op jit(solution)/shard_map/all_to_all | solution.py:48
  175.3 165.5 %all-reduce.2.cloned.1.call-start = ((), (), s32[]{:S(2)}) async-start(), calls=%async_computation.5 | async-start | bytes 368640 | tf_op jit(solution)/shard_map/psum | solution.py:55
  323.6 17.2 %copy-start.1 = (bf16[2,64,1024]{2,1,0:T(8,128)(2,1)S(1)}, bf16[2,64,1024]{2,1,0:T(8,128)(2,1)}, u32[]{:S(2)}) copy-start(bf16[2,64,1024]{2,1,0:T(8,128)(2,1)} %param.9) | copy-start | bytes 786436
  323.6 53.6 %reduce-scatter.2.cloned.1.call-start = ((), (), s32[]{:S(2)}) async-start(), calls=%async_computation.4 | async-start | bytes 1179648 | tf_op jit(solution)/shard_map/reduce_scatter | solution.py:75
  345.2 26.6 %all-to-all-start.2 = ((bf16[8,90,512]{2,1,0:T(8,128)(2,1)}), bf16[8,90,512]{2,1,0:T(8,128)(2,1)}, u32[]{:S(2)}, u32[]{:S(2)}) async-start(bf16[8,90,512]{2,1,0:T(8,128)(2,1)} %reshape.185), calls=%async_computation.3 | async-start | bytes 1572864 | tf_op jit(solution)/shard_map/all_to_all | solution.py:64
Sparse Core Ops, SparseCore 0:
  323.7 17.0 all-reduce.1
  343.1 9.4 reduce-scatter.1
where the time goes:
time: 388 us; the launch traced here: 386 us
  waiting for transfers between devices  167 us (43%)
  other arithmetic  132 us (34%)
  local copies, waits for them, and re-layouts  39.5 us (10%)
  starting transfers between devices  19.2 us (5%)
  matrix products  14.3 us (4%)
  between operations  13.6 us (4%)
    all_to_all x1, waiting for transfers between devices, local(): lax.all_to_all(outgoing, 'store', split_axis=0, concat_axis=0, tiled=True)  136 us
    sub x1, other arithmetic, local(): owners[request] * store_capacity + first_slot[request] + token_index  76.9 us
    select_n x1, other arithmetic, local(): jnp.where(filled, local_pick[request[source]], 0)  25.8 us
    all_to_all x1, waiting for transfers between devices, local(): lax.all_to_all(adapter_out.reshape(store_count_total, item_count, -1), 's...  20.7 us
    gather x2, local copies, waits for them, and re-layouts, local(): hidden_in[source]  10.9 us
    psum x1, waiting for transfers between devices, local(): chosen = lax.psum(chosen.astype(jnp.bfloat16), 'tensor').astype(jnp.float32)  10.3 us
    gather x2, other arithmetic, local(): owners[request] * store_capacity + first_slot[request] + token_index  8.9 us
  transfers between devices with their start and end apart: 5, of which 3 were waited for; matrix products, arithmetic and copies ran while one was open for 9% of the time, Pallas kernels for 0%

commit v1 on v0

v1 whole, which is shorter than its diff:
```python
import functools

import jax
import jax.numpy as jnp
from jax import lax
from jax.experimental import pallas as pl
from jax.experimental.pallas import tpu as pltpu
from jax.sharding import PartitionSpec as P

ADAPTER_SCALE = 0.5
MESH = pl.DeviceIdType.MESH
F32 = jnp.float32
BF16 = jnp.bfloat16


def adapter_of_token(lengths_row, ids_row, tokens):
    count = lengths_row.shape[1]
    down = lax.broadcasted_iota(jnp.int32, (count, count), 0)
    across = lax.broadcasted_iota(jnp.int32, (count, count), 1)
    column = jnp.sum(jnp.where(down == across, lengths_row, 0.0), axis=1, keepdims=True)
    ends = jnp.sum(jnp.where(down <= across, column, 0.0), axis=0, keepdims=True)
    starts = ends - lengths_row
    token = lax.broadcasted_iota(jnp.int32, (tokens, count), 0).astype(F32)
    inside = (token >= starts) & (token < ends)
    return jnp.sum(jnp.where(inside, ids_row, 0.0), axis=1, keepdims=True)


def kernel(
    n, x_ref, w_ref, down_ref, up_ref, len_ref, ids_ref, out_ref,
    xv, x2, wb, dv, uv, stage, big, upx, meta, metap, tok, acc, snd, rcv,
    basev, bsend, brecv,
    loc, wsem, ls, lr, pair_s, pair_r, us, ur, ss, sr,
):
    tokens = x_ref.shape[0]
    quarter = x_ref.shape[1] // 2
    adapters, _, rank = down_ref.shape
    lanes = adapters * rank
    half_out = out_ref.shape[1]
    tile = half_out // 2
    chunks = tile // 128
    requests = len_ref.shape[1]
    length = n // 2

    s = lax.axis_index("store")
    t = lax.axis_index("tensor")
    p = s // 2
    y = lax.rem(s, 2)
    sibling = {"tensor": 1 - t}
    partner = {"store": 2 * p + 1 - y}
    diagonal = {"store": 2 * p + 1 - y, "tensor": 1 - t}
    right = {"store": s + 2}
    left = {"store": s - 2}
    has_left = p > 0
    has_right = p < length - 1

    def columns(which, width):
        return pl.ds(pl.multiple_of(which * width, 128), width)

    local_down = pltpu.make_async_copy(down_ref, dv, loc.at[0])
    local_up = pltpu.make_async_copy(up_ref, uv, loc.at[1])
    local_x2 = pltpu.make_async_copy(
        x_ref.at[:, columns(y, quarter)], x2.at[pl.ds(0, tokens)], loc.at[2]
    )
    local_x = pltpu.make_async_copy(x_ref, xv, loc.at[3])
    local_down.start()
    local_up.start()

    def weight_copy(j):
        which = lax.rem((1 - t) * 2 + j, 4)
        return pltpu.make_async_copy(
            w_ref.at[:, columns(which, tile)], wb.at[j % 2], wsem.at[j]
        )

    barrier = pltpu.get_barrier_semaphore()
    for who in (sibling, partner, diagonal):
        pl.semaphore_signal(barrier, inc=1, device_id=who, device_id_type=MESH)

    @pl.when(has_left)
    def _():
        pl.semaphore_signal(barrier, inc=1, device_id=left, device_id_type=MESH)

    @pl.when(has_right)
    def _():
        pl.semaphore_signal(barrier, inc=1, device_id=right, device_id_type=MESH)

    def pack(which, dst):
        rows = pl.ds(pl.multiple_of(which * quarter, 128), quarter)
        for a in range(adapters):
            dst[0:quarter, a * rank:(a + 1) * rank] = dv[a, rows, :]
        width = columns(t * 2 + which, tile)
        for a in range(adapters):
            block = uv[a, :, width]
            for c in range(chunks):
                at = quarter + c * lanes + a * rank
                dst[at:at + rank, :] = block[:, c * 128:(c + 1) * 128]

    meta[...] = jnp.zeros_like(meta)
    meta[0:1, 0:requests] = len_ref[...]
    meta[1:2, 0:requests] = ids_ref[...]
    local_down.wait()
    local_up.wait()
    pack(1 - y, stage)

    def remote(src, dst, send, recv, who):
        return pltpu.make_async_remote_copy(
            src_ref=src, dst_ref=dst, send_sem=send, recv_sem=recv,
            device_id=who, device_id_type=MESH,
        )

    pair_block = remote(stage, big.at[2 * p + 1], pair_s.at[0], pair_r.at[0], partner)
    pair_meta = remote(meta, metap, pair_s.at[1], pair_r.at[1], partner)
    pair_x = remote(
        x_ref.at[:, columns(1 - y, quarter)], x2.at[pl.ds(tokens, tokens)],
        pair_s.at[2], pair_r.at[2], partner,
    )
    base_copy = remote(bsend, brecv, pair_s.at[3], pair_r.at[3], sibling)

    def line(direction, k, o):
        q = p - k if direction == 0 else p + k
        who = right if direction == 0 else left
        return remote(
            big.at[2 * q + o], big.at[2 * q + o],
            ls.at[direction, k, o], lr.at[direction, k, o], who,
        )

    def line_arrival(direction, k, o):
        q = p - k if direction == 0 else p + k
        return remote(
            big.at[2 * q + o], big.at[2 * q + o],
            ls.at[direction, k - 1, o], lr.at[direction, k - 1, o], partner,
        )

    def forward_up(q, o):
        slot = 2 * q + o
        return remote(
            big.at[slot, pl.ds(quarter, chunks * lanes)], upx.at[slot],
            us.at[slot], ur.at[slot], partner,
        )

    count = 3 + has_left.astype(jnp.int32) + has_right.astype(jnp.int32)
    pl.semaphore_wait(barrier, count)
    pair_block.start()
    pair_meta.start()
    pack(y, big.at[2 * p])

    def send_line(k, o, direction):
        @pl.when(has_right if direction == 0 else has_left)
        def _():
            line(direction, k, o).start()

    for direction in (0, 1):
        send_line(0, 0, direction)
    forward_up(p, 0).start()
    local_x.start()
    local_x2.start()
    weight_copy(0).start()
    weight_copy(1).start()

    lane_adapter = (lax.broadcasted_iota(jnp.int32, (1, lanes), 1) // rank).astype(F32)

    def project(q, o, first, rows):
        parity = y if o == 0 else 1 - y
        store = 2 * q + parity
        product = jnp.dot(
            x2[first:first + rows, :], big[2 * q + o, 0:quarter, :],
            preferred_element_type=F32,
        )
        wanted = lane_adapter + (store * adapters).astype(F32)
        keep = tok[first:first + rows, :] == wanted
        acc[first:first + rows, :] += jnp.where(keep, product, 0.0)

    def token_rows(ref, first):
        lengths_row = ref[0:1, 0:requests].astype(F32)
        ids_row = ref[1:2, 0:requests].astype(F32)
        tok[first:first + tokens, :] = jnp.broadcast_to(
            adapter_of_token(lengths_row, ids_row, tokens), (tokens, lanes)
        )

    acc[...] = jnp.zeros_like(acc)
    token_rows(meta, 0)
    local_x2.wait()
    project(p, 0, 0, tokens)
    pair_block.wait_recv()
    for direction in (0, 1):
        send_line(0, 1, direction)
    forward_up(p, 1).start()
    pair_block.wait_send()
    pair_x.start()
    project(p, 1, 0, tokens)

    local_x.wait()
    for j in range(4):
        weight_copy(j).wait()
        product = jnp.dot(xv[...], wb[j % 2], preferred_element_type=F32)
        at = (j % 2) * tile
        if j < 2:
            bsend[:, at:at + tile] = product.astype(BF16)
            weight_copy(j + 2).start()
        else:
            basev[:, at:at + tile] = product
        if j == 1:
            base_copy.start()

    def step(k, first, rows):
        for o in (0, 1):
            for direction in (0, 1):
                q = p - k if direction == 0 else p + k
                there = q >= 0 if direction == 0 else q < length

                @pl.when(there)
                def _():
                    line_arrival(direction, k, o).wait_recv()
                    send_line(k, o, direction)
                    forward_up(q, o).start()
                    project(q, o, first, rows)

    switch = min(2, length)

    def early(k, carry):
        step(k, 0, tokens)
        return carry

    lax.fori_loop(1, switch, early, 0)

    pair_meta.wait_recv()
    token_rows(metap, tokens)
    base_copy.wait_recv()
    basev[...] += brecv[...].astype(F32)
    pair_x.wait_recv()
    for o in (0, 1):
        project(p, o, tokens, tokens)
        for k in range(1, switch):
            for direction in (0, 1):
                q = p - k if direction == 0 else p + k
                there = q >= 0 if direction == 0 else q < length

                @pl.when(there)
                def _():
                    project(q, o, tokens, tokens)

    def late(k, carry):
        step(k, 0, 2 * tokens)
        return carry

    lax.fori_loop(switch, length, late, 0)

    snd[0] = acc[0:tokens, :].astype(BF16)
    snd[1] = acc[tokens:, :].astype(BF16)
    sums = [
        remote(snd.at[1], rcv.at[1], ss.at[1], sr.at[1], partner),
        remote(snd.at[1], rcv.at[2], ss.at[2], sr.at[2], diagonal),
        remote(snd.at[0], rcv.at[0], ss.at[0], sr.at[0], sibling),
    ]
    for copy in sums:
        copy.start()

    def wait_up(slot, carry):
        forward_up(slot // 2, lax.rem(slot, 2)).wait()
        return carry

    lax.fori_loop(0, n, wait_up, 0)
    for copy in sums:
        copy.wait_recv()
    shrink = acc[0:tokens, :]
    for i in range(3):
        shrink = shrink + rcv[i].astype(F32)

    def expand(q, carry):
        parts = []
        for o in (0, 1):
            parity = y if o == 0 else 1 - y
            wanted = lane_adapter + ((2 * q + parity) * adapters).astype(F32)
            parts.append(jnp.where(tok[0:tokens, :] == wanted, shrink, 0.0))
        left_hand = jnp.concatenate(parts, axis=1).astype(BF16)

        def columns_of(get, order):
            return jnp.concatenate(
                [
                    jnp.concatenate([get(2 * q + o, c) for o in order], axis=0)
                    for c in range(chunks)
                ],
                axis=1,
            )

        mine = columns_of(
            lambda slot, c: big[slot, quarter + c * lanes:quarter + (c + 1) * lanes, :], (0, 1)
        )
        theirs = columns_of(
            lambda slot, c: upx[slot, c * lanes:(c + 1) * lanes, :], (1, 0)
        )
        a, b = carry
        a = a + jnp.dot(left_hand, mine, preferred_element_type=F32)
        b = b + jnp.dot(left_hand, theirs, preferred_element_type=F32)
        return a, b

    zero = jnp.zeros((tokens, tile), F32)
    a, b = lax.fori_loop(0, length, expand, (zero, zero))
    for which, value in ((y, a), (1 - y, b)):
        at = columns(which, tile)
        total = basev[:, at] + ADAPTER_SCALE * value.astype(BF16).astype(F32)
        out_ref[:, at] = total.astype(BF16)

    def drain(k, carry):
        for o in (0, 1):
            @pl.when(has_right & (p - k >= 0))
            def _():
                line(0, k, o).wait_send()

            @pl.when(has_left & (p + k < length))
            def _():
                line(1, k, o).wait_send()

        return carry

    lax.fori_loop(0, length - 1, drain, 0)
    pair_meta.wait_send()
    pair_x.wait_send()
    base_copy.wait_send()
    for copy in sums:
        copy.wait_send()


def local(hidden_in, base_weight, adapter_down, adapter_up, lengths, adapter_ids):
    n = lax.axis_size("store")
    tokens, depth = hidden_in.shape
    quarter = depth // 2
    adapters, _, rank = adapter_down.shape
    lanes = adapters * rank
    width = adapter_up.shape[2]
    half = width // 2
    tile = half // 2
    up_rows = tile // 128 * lanes
    length = n // 2
    requests = lengths.shape[0]
    dma = pltpu.SemaphoreType.DMA
    vmem = pl.BlockSpec(memory_space=pltpu.VMEM)
    hbm = pl.BlockSpec(memory_space=pl.ANY)
    return pl.pallas_call(
        functools.partial(kernel, n),
        out_shape=jax.ShapeDtypeStruct((tokens, half), BF16),
        in_specs=[hbm, hbm, hbm, hbm, vmem, vmem],
        out_specs=vmem,
        scratch_shapes=[
            pltpu.VMEM((tokens, depth), BF16),
            pltpu.VMEM((2 * tokens, quarter), BF16),
            pltpu.VMEM((2, depth, tile), BF16),
            pltpu.VMEM((adapters, depth, rank), BF16),
            pltpu.VMEM((adapters, rank, width), BF16),
            pltpu.VMEM((quarter + up_rows, lanes), BF16),
            pltpu.VMEM((n, quarter + up_rows, lanes), BF16),
            pltpu.VMEM((n, up_rows, lanes), BF16),
            pltpu.VMEM((8, 128), jnp.int32),
            pltpu.VMEM((8, 128), jnp.int32),
            pltpu.VMEM((2 * tokens, lanes), F32),
            pltpu.VMEM((2 * tokens, lanes), F32),
            pltpu.VMEM((2, tokens, lanes), BF16),
            pltpu.VMEM((3, tokens, lanes), BF16),
            pltpu.VMEM((tokens, half), F32),
            pltpu.VMEM((tokens, half), BF16),
            pltpu.VMEM((tokens, half), BF16),
            dma((4,)),
            dma((4,)),
            dma((2, length, 2)),
            dma((2, length, 2)),
            dma((4,)),
            dma((4,)),
            dma((n,)),
            dma((n,)),
            dma((3,)),
            dma((3,)),
        ],
        compiler_params=pltpu.CompilerParams(
            collective_id=0, has_side_effects=True, vmem_limit_bytes=62 * 1024 * 1024
        ),
    )(
        hidden_in, base_weight, adapter_down, adapter_up,
        lengths.reshape(1, requests), adapter_ids.reshape(1, requests),
    )


def solution(mesh):
    return jax.shard_map(
        local,
        mesh=mesh,
        in_specs=(
            P(("groups", "store"), "tensor"),
            P("tensor", None),
            P(("groups", "store"), "tensor", None),
            P(("groups", "store"), None, None),
            P(("groups", "store")),
            P(("groups", "store")),
        ),
        out_specs=P(("groups", "store"), "tensor"),
        check_vma=False,
    )
```

time: 388 us -> 97.1 us (0.25)
  waiting for transfers between devices: 167 us -> 0 us
  other arithmetic: 132 us -> 0 us
  Pallas kernels: 0 us -> 91.9 us
  local copies, waits for them, and re-layouts: 39.5 us -> 4.54 us
  starting transfers between devices: 19.2 us -> 0 us
  matrix products: 14.3 us -> 0 us
  between operations: 13.6 us -> 0.01 us
    all_to_all x3 -> x0, waiting for transfers between devices: 157 us -> none  [the longest x1 136 us: local(): lax.all_to_all(outgoing, 'store', split_axis=0, concat_axis=0, tiled=True)]
    pallas_call x0 -> x1, Pallas kernels: none -> 91.9 us  [local(): pl.pallas_call(functools.partial(kernel, n), out_shape=jax.ShapeDtypeStru...]
    sub x2 -> x0, other arithmetic: 77.6 us -> none  [the longest x1 76.9 us: local(): owners[request] * store_capacity + first_slot[request] + token_index]
    select_n x6 -> x0, other arithmetic: 32.6 us -> none  [the longest x1 25.8 us: local(): jnp.where(filled, local_pick[request[source]], 0)]
    gather x16 -> x0, local copies, waits for them, and re-layouts: 27.7 us -> none  [the longest x2 10.9 us: local(): hidden_in[source]]
    all_to_all x3 -> x0, starting transfers between devices: 19.1 us -> none  [the longest x1 7.28 us: local(): lax.all_to_all(slot_labels, 'store', split_axis=0, concat_axis=0, tiled=T...]
    gather x7 -> x0, other arithmetic: 17.9 us -> none  [the longest x2 8.9 us: local(): owners[request] * store_capacity + first_slot[request] + token_index]
    dot_general x3 -> x0, matrix products: 14.3 us -> none  [the longest x1 6.8 us: local(): jnp.dot(hidden_in, base_weight, preferred_element_type=jnp.float32)]
  transfers between devices with their start and end apart: 5 -> 0, of which waited for: 3 -> 0; matrix products, arithmetic and copies ran while one was open for 9% -> 0% of each run, Pallas kernels for 0% -> 0%
where the time goes in v1:
time: 97.1 us; the launch traced here: 96.5 us
  Pallas kernels  91.9 us (95%)
  local copies, waits for them, and re-layouts  4.54 us (5%)
    pallas_call x1, Pallas kernels, local(): pl.pallas_call(functools.partial(kernel, n), out_shape=jax.ShapeDtypeStru...  91.9 us
    unnamed x2, local copies, waits for them, and re-layouts  4.54 us

profile of v1, /device:TPU:0, one launch (start us, length us, event | category | flops | bytes accessed | tf_op | source)
XLA Modules:
  0.0 96.5 jit_solution(1042566119658507063)
XLA Ops:
  0.0 2.8 %copy.7.down_ref = bf16[2,4096,64]{2,1,0:T(8,128)(2,1)} copy(bf16[2,4096,64]{1,2,0:T(8,128)(2,1)} %param.8) | data formatting | bytes 2097152 | tf_op args[2]
  2.8 91.9 %shard_map.64 = bf16[384,512]{1,0:T(8,128)(2,1)} custom-call(bf16[384,4096]{1,0:T(8,128)(2,1)} %x_ref.1, bf16[4096,1024]{1,0:T(8,128)(2,1)} %w_ref.1, bf16[2,4096,64]{2,1,0:T(8,128)(2,1)} %copy.7.down_ref, bf16[2,64,1024]{2,1,0:T(8,128)(2,1)} %up_ref.1, s32[1,48]{1,0:T(1,128)} %bitcast.2, s32[1,48]{1,0:T(1,128)} %bitcast.3), custom_call_target="tpu_custom_call" | custom-call | tf_op jit(solution)/shard_map/pallas_call | solution.py:338
  94.7 1.8 %copy.9 = bf16[384,512]{1,0:T(8,128)(2,1)} copy(bf16[384,512]{1,0:T(8,128)(2,1)} %shard_map.64) | data formatting | bytes 786432

commit v2 on v1

v2 whole, which is shorter than its diff:
```python
import functools

import jax
import jax.numpy as jnp
from jax import lax
from jax.experimental import pallas as pl
from jax.experimental.pallas import tpu as pltpu
from jax.sharding import PartitionSpec as P

ADAPTER_SCALE = 0.5
MESH = pl.DeviceIdType.MESH
F32 = jnp.float32
BF16 = jnp.bfloat16


def adapter_of_token(lengths_row, ids_row, tokens):
    count = lengths_row.shape[1]
    down = lax.broadcasted_iota(jnp.int32, (count, count), 0)
    across = lax.broadcasted_iota(jnp.int32, (count, count), 1)
    column = jnp.sum(jnp.where(down == across, lengths_row, 0.0), axis=1, keepdims=True)
    ends = jnp.sum(jnp.where(down <= across, column, 0.0), axis=0, keepdims=True)
    starts = ends - lengths_row
    token = lax.broadcasted_iota(jnp.int32, (tokens, count), 0).astype(F32)
    inside = (token >= starts) & (token < ends)
    return jnp.sum(jnp.where(inside, ids_row, 0.0), axis=1, keepdims=True)


def pack(value, rank):
    folded = value + pltpu.roll(value, rank, 1)
    rows = value.shape[0] // 2
    low = lax.broadcasted_iota(jnp.int32, (rows, 2 * rank), 1) < rank
    return jnp.where(low, folded[:rows], folded[rows:]).astype(BF16)


def unpack(value, rank):
    value = value.astype(F32)
    turned = pltpu.roll(value, rank, 1)
    low = lax.broadcasted_iota(jnp.int32, value.shape, 1) < rank
    return jnp.concatenate(
        [jnp.where(low, value, turned), jnp.where(low, turned, value)], axis=0
    )


def kernel(
    n, rank, x_ref, w_ref, down_ref, up_ref, len_ref, ids_ref, out_ref,
    xv, x2c, x2e, xe, wb, big, bigb, upx, meta, metap, metae, tok, toke, acc, acce,
    snd, rcv, snde, rcve, basev, bsend, brecv,
    loc, wsem, ls, lr, bs, br, pair_s, pair_r, us, ur, ss, sr, es, er,
):
    tokens = x_ref.shape[0]
    quarter = x_ref.shape[1] // 2
    lanes = down_ref.shape[0]
    adapters = lanes // rank
    extra = x2e.shape[1]
    common = x2c.shape[1]
    half_out = out_ref.shape[1]
    tile = half_out // 2
    requests = len_ref.shape[1]
    length = n // 2

    s = lax.axis_index("store")
    t = lax.axis_index("tensor")
    p = s // 2
    y = lax.rem(s, 2)
    sibling = {"tensor": 1 - t}
    partner = {"store": 2 * p + 1 - y}
    diagonal = {"store": 2 * p + 1 - y, "tensor": 1 - t}
    right = {"store": s + 2}
    left = {"store": s - 2}
    has_left = p > 0
    has_right = p < length - 1
    is_end = (p == 0) | (p == length - 1)
    is_inner = (p > 0) & (p < length - 1)
    is_helper = (p == 1) | (p == length - 2)
    peer = {"store": s + jnp.where((p == 0) | (p == length - 2), 2, -2)}

    def columns(which, width):
        return pl.ds(pl.multiple_of(which * width, 128), width)

    def common_of(which):
        return pl.ds(pl.multiple_of(which * quarter, 128), common)

    def extra_of(which):
        return pl.ds(pl.multiple_of(which * quarter + common, 128), extra)

    own_rows = pl.ds(0, tokens)
    other_rows = pl.ds(tokens, tokens)
    down_part = (slice(None), pl.ds(0, common))
    up_part = (slice(None), pl.ds(common, tile))

    def local_copy(src, dst, i):
        return pltpu.make_async_copy(src, dst, loc.at[i])

    local_a = local_copy(down_ref.at[:, common_of(y)], big.at[(2 * p,) + down_part], 0)
    local_u = local_copy(up_ref.at[:, columns(t * 2 + y, tile)], big.at[(2 * p,) + up_part], 1)
    local_b = local_copy(down_ref.at[:, extra_of(y)], bigb.at[2 * p], 2)
    local_xe = local_copy(x_ref.at[:, extra_of(y)], x2e.at[own_rows], 3)
    local_xc = local_copy(x_ref.at[:, common_of(y)], x2c.at[own_rows], 4)
    local_x = local_copy(x_ref, xv, 5)

    def weight_copy(j):
        which = lax.rem((1 - t) * 2 + j, 4)
        return pltpu.make_async_copy(
            w_ref.at[:, columns(which, tile)], wb.at[j % 2], wsem.at[j]
        )

    barrier = pltpu.get_barrier_semaphore()
    for who in (sibling, partner, diagonal):
        pl.semaphore_signal(barrier, inc=1, device_id=who, device_id_type=MESH)

    @pl.when(has_left)
    def _():
        pl.semaphore_signal(barrier, inc=1, device_id=left, device_id_type=MESH)

    @pl.when(has_right)
    def _():
        pl.semaphore_signal(barrier, inc=1, device_id=right, device_id_type=MESH)

    for copy in (local_a, local_u, local_b, local_xe, local_xc, local_x):
        copy.start()
    weight_copy(0).start()
    weight_copy(1).start()
    meta[...] = jnp.zeros_like(meta)
    meta[0:1, 0:requests] = len_ref[...]
    meta[1:2, 0:requests] = ids_ref[...]

    def remote(src, dst, send, recv, who):
        return pltpu.make_async_remote_copy(
            src_ref=src, dst_ref=dst, send_sem=send, recv_sem=recv,
            device_id=who, device_id_type=MESH,
        )

    def pair_copy(src, dst, i, who=partner):
        return remote(src, dst, pair_s.at[i], pair_r.at[i], who)

    pair_a = pair_copy(down_ref.at[:, common_of(1 - y)], big.at[(2 * p + 1,) + down_part], 0)
    pair_u = pair_copy(
        up_ref.at[:, columns(t * 2 + 1 - y, tile)], big.at[(2 * p + 1,) + up_part], 1
    )
    pair_meta = pair_copy(meta, metap, 2)
    pair_xe = pair_copy(x_ref.at[:, extra_of(1 - y)], x2e.at[other_rows], 3)
    pair_b = pair_copy(down_ref.at[:, extra_of(1 - y)], bigb.at[2 * p + 1], 4)
    pair_xc = pair_copy(x_ref.at[:, common_of(1 - y)], x2c.at[other_rows], 5)
    base_copy = pair_copy(bsend, brecv, 6, sibling)

    def end_copy(src, dst, i):
        return remote(src, dst, es.at[i], er.at[i], peer)

    end_x = [
        end_copy(x2e.at[own_rows], xe.at[own_rows], 0),
        end_copy(x2e.at[other_rows], xe.at[other_rows], 1),
    ]
    end_meta = [end_copy(meta, metae.at[0], 2), end_copy(metap, metae.at[1], 3)]
    end_sum = end_copy(snde, rcve, 4)

    def position(direction, k):
        return p - k if direction == 0 else p + k

    def inside(direction, k):
        return position(direction, k) >= 0 if direction == 0 else position(direction, k) < length

    def line(buffer, send, recv, direction, k, o):
        slot = buffer.at[2 * position(direction, k) + o]
        return remote(
            slot, slot, send.at[direction, k, o], recv.at[direction, k, o],
            right if direction == 0 else left,
        )

    def arrival(buffer, send, recv, direction, k, o):
        slot = buffer.at[2 * position(direction, k) + o]
        return remote(
            slot, slot, send.at[direction, k - 1, o], recv.at[direction, k - 1, o], partner
        )

    goes = (has_right, has_left)
    goes_b = (p < length - 2, p > 1)

    def send_a(k, o, direction):
        @pl.when(goes[direction])
        def _():
            line(big, ls, lr, direction, k, o).start()

    def send_b(k, o, direction):
        @pl.when(goes_b[direction])
        def _():
            line(bigb, bs, br, direction, k, o).start()

    def forward_up(slot):
        return remote(big.at[(slot,) + up_part], upx.at[slot], us.at[slot], ur.at[slot], partner)

    lane_adapter = (lax.broadcasted_iota(jnp.int32, (1, lanes), 1) // rank).astype(F32)

    def wanted(q, o):
        store = 2 * q + (y if o == 0 else 1 - y)
        return lane_adapter + (store * adapters).astype(F32)

    def product(q, x, buffer, width, adapter):
        weights = buffer[pl.ds(2 * q, 2), :, 0:width].reshape(2 * lanes, width)
        full = lax.dot_general(
            x, weights, (((1,), (1,)), ((), ())), preferred_element_type=F32
        )
        return jnp.where(adapter == wanted(q, 0), full[:, 0:lanes], 0.0) + jnp.where(
            adapter == wanted(q, 1), full[:, lanes:], 0.0
        )

    def project_a(q, first):
        rows = slice(first, first + tokens)
        acc[rows, :] += product(q, x2c[rows, :], big, common, tok[rows, :])

    def project_b(q, first):
        rows = slice(first, first + tokens)
        acc[rows, :] += product(q, x2e[rows, :], bigb, extra, tok[rows, :])

    def token_rows(ref, dst, first):
        lengths_row = ref[0:1, 0:requests].astype(F32)
        ids_row = ref[1:2, 0:requests].astype(F32)
        dst[first:first + tokens, :] = jnp.broadcast_to(
            adapter_of_token(lengths_row, ids_row, tokens), (tokens, lanes)
        )

    count = 3 + has_left.astype(jnp.int32) + has_right.astype(jnp.int32)
    pl.semaphore_wait(barrier, count)
    pair_a.start()
    pair_u.start()
    pair_meta.start()
    local_a.wait()
    local_u.wait()
    for direction in (0, 1):
        send_a(0, 0, direction)
    forward_up(2 * p).start()
    acc[...] = jnp.zeros_like(acc)
    token_rows(meta, tok, 0)
    local_b.wait()
    local_xe.wait()
    local_xc.wait()
    pair_a.wait_recv()
    pair_u.wait_recv()
    for direction in (0, 1):
        send_a(0, 1, direction)
    forward_up(2 * p + 1).start()
    pair_a.wait_send()
    pair_u.wait_send()
    pair_xe.start()

    @pl.when(is_end)
    def _():
        end_meta[0].start()
        end_x[0].start()

    project_a(p, 0)

    local_x.wait()
    for j in range(4):
        weight_copy(j).wait()
        part = jnp.dot(xv[...], wb[j % 2], preferred_element_type=F32)
        at = (j % 2) * tile
        if j < 2:
            bsend[:, at:at + tile] = part.astype(BF16)
            weight_copy(j + 2).start()
        else:
            basev[:, at:at + tile] = part
        if j == 1:
            base_copy.start()

    def step_a(k):
        for o in (0, 1):
            for direction in (0, 1):
                @pl.when(inside(direction, k))
                def _():
                    arrival(big, ls, lr, direction, k, o).wait_recv()
                    send_a(k, o, direction)
                    forward_up(2 * position(direction, k) + o).start()

        for direction in (0, 1):
            @pl.when(inside(direction, k))
            def _():
                project_a(position(direction, k), 0)

    step_a(1)
    pair_xe.wait_send()
    pair_b.start()
    pair_xc.start()
    pair_meta.wait_recv()
    token_rows(metap, tok, tokens)
    base_copy.wait_recv()
    basev[...] += brecv[...].astype(F32)
    pair_xe.wait_recv()

    @pl.when(is_end)
    def _():
        for direction in (0, 1):
            send_b(0, 0, direction)
        end_meta[1].start()
        end_x[1].start()

    pair_b.wait_recv()

    @pl.when(is_end)
    def _():
        for direction in (0, 1):
            send_b(0, 1, direction)

    def loop_a(k, carry):
        step_a(k)
        return carry

    lax.fori_loop(2, length, loop_a, 0)

    @pl.when(is_inner)
    def _():
        for o in (0, 1):
            for direction in (0, 1):
                send_b(0, o, direction)
        project_b(p, 0)

        def loop_b(k, carry):
            for o in (0, 1):
                for direction in (0, 1):
                    @pl.when(inside(direction, k))
                    def _():
                        arrival(bigb, bs, br, direction, k, o).wait_recv()
                        send_b(k, o, direction)

            for direction in (0, 1):
                @pl.when(inside(direction, k))
                def _():
                    project_b(position(direction, k), 0)

            return carry

        lax.fori_loop(1, length - 1, loop_b, 0)

    @pl.when(is_helper)
    def _():
        for copy in end_meta + end_x:
            copy.wait_recv()
        for i in (0, 1):
            token_rows(metae.at[i], toke, i * tokens)
        acce[...] = jnp.zeros_like(acce)

        def loop_e(q, carry):
            acce[...] += product(q, xe[...], bigb, extra, toke[...])
            return carry

        lax.fori_loop(0, length, loop_e, 0)
        for i in (0, 1):
            snde[i] = pack(acce[i * tokens:(i + 1) * tokens, :], rank)
        end_sum.start()

    pair_xc.wait_recv()

    def loop_partner(q, carry):
        project_a(q, tokens)

        @pl.when(is_inner)
        def _():
            project_b(q, tokens)

        return carry

    lax.fori_loop(0, length, loop_partner, 0)

    @pl.when(is_end)
    def _():
        end_sum.wait_recv()
        for i in (0, 1):
            rows = slice(i * tokens, (i + 1) * tokens)
            parity = tok[rows, :] - 2.0 * jnp.floor(tok[rows, :] * 0.5)
            acc[rows, :] += jnp.where(parity == lane_adapter, unpack(rcve[i], rank), 0.0)

    snd[1] = pack(acc[tokens:, :], rank)
    snd[0] = pack(acc[0:tokens, :], rank)
    sums = [
        remote(snd.at[1], rcv.at[2], ss.at[2], sr.at[2], diagonal),
        remote(snd.at[1], rcv.at[1], ss.at[1], sr.at[1], partner),
        remote(snd.at[0], rcv.at[0], ss.at[0], sr.at[0], sibling),
    ]
    for copy in sums:
        copy.start()

    def wait_up(slot, carry):
        forward_up(slot).wait()
        return carry

    lax.fori_loop(0, n, wait_up, 0)
    for copy in sums:
        copy.wait_recv()
    shrink = acc[0:tokens, :]
    for i in range(3):
        shrink = shrink + unpack(rcv[i], rank)
    own_adapter = tok[0:tokens, :]

    def expand(q, carry):
        parts = [jnp.where(own_adapter == wanted(q, o), shrink, 0.0) for o in (0, 1)]
        rows = jnp.concatenate(parts, axis=1).astype(BF16)
        mine = big[pl.ds(2 * q, 2), :, common:common + tile].reshape(2 * lanes, tile)
        theirs = jnp.concatenate([upx[2 * q + 1], upx[2 * q]], axis=0)
        a, b = carry
        a = a + jnp.dot(rows, mine, preferred_element_type=F32)
        b = b + jnp.dot(rows, theirs, preferred_element_type=F32)
        return a, b

    zero = jnp.zeros((tokens, tile), F32)
    a, b = lax.fori_loop(0, length, expand, (zero, zero))
    for which, value in ((y, a), (1 - y, b)):
        at = columns(which, tile)
        total = basev[:, at] + ADAPTER_SCALE * value.astype(BF16).astype(F32)
        out_ref[:, at] = total.astype(BF16)

    def drain(k, carry):
        for o in (0, 1):
            for direction in (0, 1):
                @pl.when(goes[direction] & inside(direction, k))
                def _():
                    line(big, ls, lr, direction, k, o).wait_send()

                @pl.when(goes_b[direction] & inside(direction, k))
                def _():
                    line(bigb, bs, br, direction, k, o).wait_send()

        return carry

    lax.fori_loop(0, length - 1, drain, 0)

    @pl.when(is_end)
    def _():
        for copy in end_meta + end_x:
            copy.wait_send()

    @pl.when(is_helper)
    def _():
        end_sum.wait_send()

    for copy in [pair_meta, pair_b, pair_xc, base_copy] + sums:
        copy.wait_send()


def local(hidden_in, base_weight, adapter_down, adapter_up, lengths, adapter_ids):
    n = lax.axis_size("store")
    tokens, depth = hidden_in.shape
    quarter = depth // 2
    adapters, _, rank = adapter_down.shape
    lanes = adapters * rank
    width = adapter_up.shape[2]
    half = width // 2
    tile = half // 2
    length = n // 2
    assert length >= 4 and adapters == 2
    extra = quarter * 3 // 8 // 128 * 128
    common = quarter - extra
    requests = lengths.shape[0]
    dma = pltpu.SemaphoreType.DMA
    vmem = pl.BlockSpec(memory_space=pltpu.VMEM)
    hbm = pl.BlockSpec(memory_space=pl.ANY)
    return pl.pallas_call(
        functools.partial(kernel, n, rank),
        out_shape=jax.ShapeDtypeStruct((tokens, half), BF16),
        in_specs=[hbm, hbm, hbm, hbm, vmem, vmem],
        out_specs=vmem,
        scratch_shapes=[
            pltpu.VMEM((tokens, depth), BF16),
            pltpu.VMEM((2 * tokens, common), BF16),
            pltpu.VMEM((2 * tokens, extra), BF16),
            pltpu.VMEM((2 * tokens, extra), BF16),
            pltpu.VMEM((2, depth, tile), BF16),
            pltpu.VMEM((n, lanes, common + tile), BF16),
            pltpu.VMEM((n, lanes, extra), BF16),
            pltpu.VMEM((n, lanes, tile), BF16),
            pltpu.VMEM((8, 128), jnp.int32),
            pltpu.VMEM((8, 128), jnp.int32),
            pltpu.VMEM((2, 8, 128), jnp.int32),
            pltpu.VMEM((2 * tokens, lanes), F32),
            pltpu.VMEM((2 * tokens, lanes), F32),
            pltpu.VMEM((2 * tokens, lanes), F32),
            pltpu.VMEM((2 * tokens, lanes), F32),
            pltpu.VMEM((2, tokens // 2, lanes), BF16),
            pltpu.VMEM((3, tokens // 2, lanes), BF16),
            pltpu.VMEM((2, tokens // 2, lanes), BF16),
            pltpu.VMEM((2, tokens // 2, lanes), BF16),
            pltpu.VMEM((tokens, half), F32),
            pltpu.VMEM((tokens, half), BF16),
            pltpu.VMEM((tokens, half), BF16),
            dma((6,)),
            dma((4,)),
            dma((2, length, 2)),
            dma((2, length, 2)),
            dma((2, length, 2)),
            dma((2, length, 2)),
            dma((7,)),
            dma((7,)),
            dma((n,)),
            dma((n,)),
            dma((3,)),
            dma((3,)),
            dma((5,)),
            dma((5,)),
        ],
        compiler_params=pltpu.CompilerParams(
            collective_id=0, has_side_effects=True, vmem_limit_bytes=62 * 1024 * 1024
        ),
    )(
        hidden_in, base_weight,
        adapter_down.transpose(0, 2, 1).reshape(lanes, depth),
        adapter_up.reshape(lanes, width),
        lengths.reshape(1, requests), adapter_ids.reshape(1, requests),
    )


def solution(mesh):
    return jax.shard_map(
        local,
        mesh=mesh,
        in_specs=(
            P(("groups", "store"), "tensor"),
            P("tensor", None),
            P(("groups", "store"), "tensor", None),
            P(("groups", "store"), None, None),
            P(("groups", "store")),
            P(("groups", "store")),
        ),
        out_specs=P(("groups", "store"), "tensor"),
        check_vma=False,
    )
```

time: 97.1 us -> 80.2 us (0.83)
  Pallas kernels: 91.9 us -> 78.3 us
  local copies, waits for them, and re-layouts: 4.54 us -> 1.77 us
    pallas_call x1, Pallas kernels: 91.9 us -> 78.3 us  [local(): pl.pallas_call(functools.partial(kernel, n, rank), out_shape=jax.ShapeDty...]
    unnamed x2 -> x1, local copies, waits for them, and re-layouts: 4.54 us -> 1.77 us
where the time goes in v2:
time: 80.2 us; the launch traced here: 80.1 us
  Pallas kernels  78.3 us (98%)
  local copies, waits for them, and re-layouts  1.77 us (2%)
    pallas_call x1, Pallas kernels, local(): pl.pallas_call(functools.partial(kernel, n, rank), out_shape=jax.ShapeDty...  78.3 us
    unnamed x1, local copies, waits for them, and re-layouts  1.77 us

profile of v2, /device:TPU:0, one launch (start us, length us, event | category | flops | bytes accessed | tf_op | source)
XLA Modules:
  0.0 80.1 jit_solution(3264153792184516107)
XLA Ops:
  0.0 78.3 %shard_map.64 = bf16[384,512]{1,0:T(8,128)(2,1)} custom-call(bf16[384,4096]{1,0:T(8,128)(2,1)} %x_ref.1, bf16[4096,1024]{1,0:T(8,128)(2,1)} %w_ref.1, bf16[128,4096]{1,0:T(8,128)(2,1)} %bitcast.6, bf16[128,1024]{1,0:T(8,128)(2,1)} %bitcast.7, s32[1,48]{1,0:T(1,128)} %bitcast.8, s32[1,48]{1,0:T(1,128)} %bitcast.9), custom_call_target="tpu_custom_call" | custom-call | tf_op jit(solution)/shard_map/pallas_call | solution.py:455
  78.3 1.8 %copy.8 = bf16[384,512]{1,0:T(8,128)(2,1)} copy(bf16[384,512]{1,0:T(8,128)(2,1)} %shard_map.64) | data formatting | bytes 786432

commit v3 on v2

--- a/solution.py
+++ b/solution.py
@@ -240,13 +240,8 @@
     forward_up(2 * p + 1).start()
     pair_a.wait_send()
     pair_u.wait_send()
+    pair_b.start()
     pair_xe.start()
-
-    @pl.when(is_end)
-    def _():
-        end_meta[0].start()
-        end_x[0].start()
-
     project_a(p, 0)
 
     local_x.wait()
@@ -276,9 +271,21 @@
             def _():
                 project_a(position(direction, k), 0)
 
+    @pl.when(is_end)
+    def _():
+        end_meta[0].start()
+        end_x[0].start()
+
     step_a(1)
+    pair_b.wait_recv()
+
+    @pl.when(is_end)
+    def _():
+        for o in (0, 1):
+            for direction in (0, 1):
+                send_b(0, o, direction)
+
     pair_xe.wait_send()
-    pair_b.start()
     pair_xc.start()
     pair_meta.wait_recv()
     token_rows(metap, tok, tokens)
@@ -288,17 +295,8 @@
 
     @pl.when(is_end)
     def _():
-        for direction in (0, 1):
-            send_b(0, 0, direction)
         end_meta[1].start()
         end_x[1].start()
-
-    pair_b.wait_recv()
-
-    @pl.when(is_end)
-    def _():
-        for direction in (0, 1):
-            send_b(0, 1, direction)
 
     def loop_a(k, carry):
         step_a(k)
@@ -446,7 +444,7 @@
     tile = half // 2
     length = n // 2
     assert length >= 4 and adapters == 2
-    extra = quarter * 3 // 8 // 128 * 128
+    extra = quarter * 5 // 16 // 128 * 128
     common = quarter - extra
     requests = lengths.shape[0]
     dma = pltpu.SemaphoreType.DMA

time: 80.2 us -> 75.3 us (0.939)
  Pallas kernels: 78.3 us -> 73.4 us
    pallas_call x1, Pallas kernels: 78.3 us -> 73.4 us  [local(): pl.pallas_call(functools.partial(kernel, n, rank), out_shape=jax.ShapeDty...]
where the time goes in v3:
time: 75.3 us; the launch traced here: 75.2 us
  Pallas kernels  73.4 us (97%)
  local copies, waits for them, and re-layouts  1.77 us (2%)
    pallas_call x1, Pallas kernels, local(): pl.pallas_call(functools.partial(kernel, n, rank), out_shape=jax.ShapeDty...  73.4 us
    unnamed x1, local copies, waits for them, and re-layouts  1.77 us

profile of v3, /device:TPU:0, one launch (start us, length us, event | category | flops | bytes accessed | tf_op | source)
XLA Modules:
  0.0 75.2 jit_solution(18097896139875458054)
XLA Ops:
  0.0 73.4 %shard_map.64 = bf16[384,512]{1,0:T(8,128)(2,1)} custom-call(bf16[384,4096]{1,0:T(8,128)(2,1)} %x_ref.1, bf16[4096,1024]{1,0:T(8,128)(2,1)} %w_ref.1, bf16[128,4096]{1,0:T(8,128)(2,1)} %bitcast.6, bf16[128,1024]{1,0:T(8,128)(2,1)} %bitcast.7, s32[1,48]{1,0:T(1,128)} %bitcast.8, s32[1,48]{1,0:T(1,128)} %bitcast.9), custom_call_target="tpu_custom_call" | custom-call | tf_op jit(solution)/shard_map/pallas_call | solution.py:453
  73.4 1.8 %copy.8 = bf16[384,512]{1,0:T(8,128)(2,1)} copy(bf16[384,512]{1,0:T(8,128)(2,1)} %shard_map.64) | data formatting | bytes 786432

commit v4 on v3

--- a/solution.py
+++ b/solution.py
@@ -278,12 +278,9 @@
 
     step_a(1)
     pair_b.wait_recv()
-
-    @pl.when(is_end)
-    def _():
-        for o in (0, 1):
-            for direction in (0, 1):
-                send_b(0, o, direction)
+    for o in (0, 1):
+        for direction in (0, 1):
+            send_b(0, o, direction)
 
     pair_xe.wait_send()
     pair_xc.start()
@@ -306,9 +303,6 @@
 
     @pl.when(is_inner)
     def _():
-        for o in (0, 1):
-            for direction in (0, 1):
-                send_b(0, o, direction)
         project_b(p, 0)
 
         def loop_b(k, carry):

time: 75.3 us -> 74.8 us (level)
  no operation moved by 1% of the time
where the time goes in v4:
time: 74.8 us; the launch traced here: 74.6 us
  Pallas kernels  72.8 us (97%)
  local copies, waits for them, and re-layouts  1.77 us (2%)
    pallas_call x1, Pallas kernels, local(): pl.pallas_call(functools.partial(kernel, n, rank), out_shape=jax.ShapeDty...  72.8 us
    unnamed x1, local copies, waits for them, and re-layouts  1.77 us

profile of v4, /device:TPU:0, one launch (start us, length us, event | category | flops | bytes accessed | tf_op | source)
XLA Modules:
  0.0 74.6 jit_solution(9297300941701188617)
XLA Ops:
  0.0 72.8 %shard_map.64 = bf16[384,512]{1,0:T(8,128)(2,1)} custom-call(bf16[384,4096]{1,0:T(8,128)(2,1)} %x_ref.1, bf16[4096,1024]{1,0:T(8,128)(2,1)} %w_ref.1, bf16[128,4096]{1,0:T(8,128)(2,1)} %bitcast.6, bf16[128,1024]{1,0:T(8,128)(2,1)} %bitcast.7, s32[1,48]{1,0:T(1,128)} %bitcast.8, s32[1,48]{1,0:T(1,128)} %bitcast.9), custom_call_target="tpu_custom_call" | custom-call | tf_op jit(solution)/shard_map/pallas_call | solution.py:447
  72.8 1.8 %copy.8 = bf16[384,512]{1,0:T(8,128)(2,1)} copy(bf16[384,512]{1,0:T(8,128)(2,1)} %shard_map.64) | data formatting | bytes 786432
